TPU v7x, 512 devices: a whole 4x4x16 slice. The times are simulated.
512 devices in a mesh: pts: 64 (over z, x), cen: 8 (over y, core).
Axes of the slice: x: 4, y: 4, z: 16, core: 2. Of those that a mesh axis runs over, the one named last changes fastest.
Arguments:
- points: bfloat16 [65536, 1024], P('pts'), may hold values from -24 to 24
- centroids_t: bfloat16 [1024, 8192], P('pts', 'cen'), may hold values from -0.15 to 0.15
Outputs:
- new_centroids: float32 [1024, 8192], P('pts', 'cen')
- assignments: bfloat16 [65536, 8192], P('pts', 'cen')
All inputs are finite; a program needn't handle non-finite values.
Results may differ from a plain program's by a relative error of at most 0.002.
Values may be sent and summed in bfloat16 or wider, within the bound.
A program may use at most 64 MiB of HBM per device.

v0:
```python
import jax
import jax.numpy as jnp
from jax import lax
from jax.sharding import PartitionSpec as P

PASSES = 3


smoothing_scale_factor = 0.8


def column_totals(masses):
    return lax.psum(jnp.sum(masses, axis=0), "pts")


def row_balance(masses):
    return lax.psum(jnp.sum(masses, axis=1), "cen")


def on_device(points, centroids_t):
    piece = lax.all_gather(centroids_t, "pts", axis=0, tiled=True)
    columns = points
    product_running_sum = jnp.dot(columns, piece, preferred_element_type=jnp.float32)
    accrued_length_tally = jnp.sum(jnp.square(piece.astype(jnp.float32)), axis=0)
    cluster_score_matrix = (
        2.0 * product_running_sum - accrued_length_tally[None, :]
    ) / smoothing_scale_factor
    line_highest_entry = lax.pmax(jnp.max(cluster_score_matrix, axis=1), "cen")
    weights = jnp.exp(cluster_score_matrix - line_highest_entry[:, None])
    row_sum = lax.psum(jnp.sum(weights, axis=1), "cen")
    transport = weights / row_sum[:, None]
    for repeat_index in range(PASSES):
        transport = transport / column_totals(transport)[None, :]
        transport = transport / row_balance(transport)[:, None]
    assignments = transport.astype(jnp.bfloat16)
    counts = lax.psum(jnp.sum(assignments, axis=0, dtype=jnp.float32), "pts")
    columns = points
    numerators = lax.psum_scatter(
        lax.dot_general(
            columns, assignments, (((0,), (0,)), ((), ())), preferred_element_type=jnp.float32
        ),
        "pts",
        scatter_dimension=0,
        tiled=True,
    )
    return (numerators / counts[None, :], assignments)


def solution(mesh):
    return jax.shard_map(
        on_device,
        mesh=mesh,
        in_specs=(P("pts", None), P("pts", "cen")),
        out_specs=(P("pts", "cen"), P("pts", "cen")),
        check_vma=False,
    )
```

profile of v0, /device:TPU:8, one launch (start us, length us, event | category | flops | bytes accessed | tf_op | source)
XLA Modules:
  0.0 1386.3 jit_solution(9271761769310216923)
XLA Ops:
  7.2 0.0 copy-start
  7.2 0.0 all-gather.2.cloned.1.call-start
  7.2 0.7 all-gather.2.cloned.1.call-update
  7.9 0.0 reduce-scatter.4.cloned.1.call-start
  8.0 148.4 %all-gather.2.cloned.1.call-done = bf16[1024,1024]{1,0:T(8,128)(2,1)} async-done(((bf16[16,1024]{1,0:T(8,128)(2,1)}), bf16[1024,1024]{1,0:T(8,128)(2,1)}) %all-gather.2.cloned.1.call-update) | async-done | bytes 2097168 | tf_op jit(solution)/shard_map/all_gather | solution.py:21
  156.3 2.1 multiply_reduce_fusion
  158.4 0.0 copy-done
  158.4 6.1 fusion.15
  164.5 10.0 pmax.7
  174.5 3.2 fusion.16
  177.7 12.4 psum.56
  190.1 3.5 divide_reduce_fusion
  193.6 141.4 %psum.57 = f32[1024]{0:T(1024)S(1)} all-reduce(f32[1024]{0:T(1024)S(1)} %divide_reduce_fusion), channel_id=1, replica_groups=mesh['pts'=64,'cen'=8] {'pts'}, use_global_device_ids=true, to_apply=%region_6.0 | all-reduce | flops 1024 | bytes 8192 | tf_op jit(solution)/shard_map/psum | solution.py:13
  335.1 3.2 fusion.9
  338.2 11.9 psum.58
  350.1 3.8 fusion.11
  353.9 138.0 %psum.59 = f32[1024]{0:T(1024)S(1)} all-reduce(f32[1024]{0:T(1024)S(1)} %fusion.11), channel_id=1, replica_groups=mesh['pts'=64,'cen'=8] {'pts'}, use_global_device_ids=true, to_apply=%region_10.0 | all-reduce | flops 1024 | bytes 8192 | tf_op jit(solution)/shard_map/psum | solution.py:13
  491.9 3.5 fusion.12
  495.4 12.4 psum.60
  507.8 4.0 fusion.13
  511.8 140.0 %psum.61 = f32[1024]{0:T(1024)S(1)} all-reduce(f32[1024]{0:T(1024)S(1)} %fusion.13), channel_id=1, replica_groups=mesh['pts'=64,'cen'=8] {'pts'}, use_global_device_ids=true, to_apply=%region_14.0 | all-reduce | flops 1024 | bytes 8192 | tf_op jit(solution)/shard_map/psum | solution.py:13
  651.8 3.7 fusion.14
  655.5 12.6 psum.62
  668.1 4.4 convert_reduce_fusion
  672.5 0.0 copy-start.1
  672.5 1.4 copy-done.1
  673.9 4.3 convolution_bitcast_fusion
  678.2 5.3 copy.8
  683.6 0.0 reduce-scatter.4.cloned.1.call-update
  683.6 3.9 copy.7
  687.5 138.1 %psum.63 = f32[1024]{0:T(1024)S(1)} all-reduce(f32[1024]{0:T(1024)S(1)} %get-tuple-element.6), channel_id=1, replica_groups=mesh['pts'=64,'cen'=8] {'pts'}, use_global_device_ids=true, to_apply=%region_19.0 | all-reduce | flops 1024 | bytes 8192 | tf_op jit(solution)/shard_map/psum | solution.py:36
  825.7 551.8 %reduce-scatter.4.cloned.1.call-done = f32[16,1024]{1,0:T(8,128)} async-done(((f32[1024,1024]{1,0:T(8,128)}), f32[16,1024]{1,0:T(8,128)}) %reduce-scatter.4.cloned.1.call-update) | async-done | bytes 65552
  1377.4 1.0 copy.9
  1378.5 0.2 broadcast_divide_fusion
  1378.7 0.8 copy.6
Async XLA Ops:
  7.2 151.2 %copy-start = (bf16[1024,1024]{1,0:T(8,128)(2,1)S(1)}, bf16[1024,1024]{1,0:T(8,128)(2,1)}, u32[]{:S(2)}) copy-start(bf16[1024,1024]{1,0:T(8,128)(2,1)} %param.2) | copy-start | bytes 6291460
  7.2 149.1 %all-gather.2.cloned.1.call-start = ((), (), s32[]{:S(2)}) async-start(), calls=%async_computation.1 | async-start | bytes 2129920 | tf_op jit(solution)/shard_map/all_gather | solution.py:21
  7.9 1369.5 %reduce-scatter.4.cloned.1.call-start = ((), (), s32[]{:S(2)}) async-start(), calls=%async_computation.2 | async-start | bytes 4259840
  672.5 1.4 copy-start.1
Sparse Core Ops, SparseCore 0:
  11.0 145.3 all-gather.1
  683.7 693.6 reduce-scatter.3
where the time goes:
time: 1390 us
  waiting for transfers between devices  701 us (50%)
  blocking collectives  617 us (44%)
  other arithmetic  31.5 us (2%)
  between operations  14.1 us (1%)
    unnamed x3, waiting for transfers between devices  552 us
    psum x3, blocking collectives, column_totals(): return lax.psum(jnp.sum(masses, axis=0), 'pts')  419 us
    all_gather x1, waiting for transfers between devices, on_device(): piece = lax.all_gather(centroids_t, 'pts', axis=0, tiled=True)  148 us
    psum x1, blocking collectives, on_device(): counts = lax.psum(jnp.sum(assignments, axis=0, dtype=jnp.float32), 'pts')  138 us
    psum x3, blocking collectives, row_balance(): return lax.psum(jnp.sum(masses, axis=1), 'cen')  37 us
  transfers between devices with their start and end apart: 2, of which 2 were waited for; matrix products, arithmetic and copies ran while one was open for 0% of the time, Pallas kernels for 0%

commit v1 on v0

v1 whole, which is shorter than its diff:
```python
import functools

import jax
import jax.numpy as jnp
from jax import lax
from jax.experimental import pallas as pl
from jax.experimental.pallas import tpu as pltpu
from jax.sharding import PartitionSpec as P

PASSES = 3
MESH = pl.DeviceIdType.MESH
L = 128
F32 = jnp.float32
BF16 = jnp.bfloat16
X_CHIPS = 4
Z_GROUP = 2


def kernel(nx, nz, nc, za, points_ref, cent_ref, newc_ref, assign_ref,
           pts, pts_t, piece, mass, top, assign, own, xsend, xrecv, zsend, zrecv,
           soft, rows, cols_a, cols_b,
           local_sem, gx_send, gx_recv, gz_send, gz_recv, soft_send, soft_recv,
           row_send, row_recv, ca_send, ca_recv, cb_send, cb_recv,
           rx_send, rx_recv, rz_send, rz_recv):
    n_rows, n_d = points_ref.shape
    chunk, n_k = cent_ref.shape
    row_blocks = n_rows // L
    col_tiles = n_k // L
    wide = min(256, n_k)
    zb = nz // za
    na = za * nx
    right_steps = nz // 2
    left_steps = nz - 1 - right_steps

    p = lax.axis_index("pts")
    c = lax.axis_index("cen")
    z = p // nx
    x = p % nx
    ga = (z % za) * nx + x
    gb = z // za

    def cen_peer(o):
        return {"cen": (c + o) % nc}

    def a_peer(o):
        q = (ga + o) % na
        return {"pts": ((z // za) * za + q // nx) * nx + q % nx}

    def b_peer(o):
        return {"pts": (((gb + o) % zb) * za + z % za) * nx + x}

    def x_peer(o):
        return {"pts": z * nx + (x + o) % nx}

    def z_peer(o):
        return {"pts": ((z + nz + o) % nz) * nx + x}

    load = pltpu.make_async_copy(points_ref, pts, local_sem.at[0])
    load.start()

    barrier = pltpu.get_barrier_semaphore()

    def greet(peer, n):
        def body(o, carry):
            pl.semaphore_signal(barrier, inc=1, device_id=peer(o), device_id_type=MESH)
            return carry
        lax.fori_loop(1, n, body, 0)

    greet(cen_peer, nc)
    greet(a_peer, na)
    greet(b_peer, zb)
    pl.semaphore_signal(barrier, inc=1, device_id=z_peer(1), device_id_type=MESH)
    pl.semaphore_signal(barrier, inc=1, device_id=z_peer(-1), device_id_type=MESH)
    pl.semaphore_wait(barrier, (nc - 1) + (na - 1) + (zb - 1) + 2)

    def slab(first, n):
        return piece.at[pl.ds(pl.multiple_of(first * chunk, chunk), n * chunk), :]

    piece[pl.ds(pl.multiple_of(p * chunk, chunk), chunk), :] = cent_ref[...]

    def gx(o):
        return pltpu.make_async_remote_copy(
            src_ref=slab(p, 1), dst_ref=slab(p, 1), send_sem=gx_send.at[o], recv_sem=gx_recv.at[o],
            device_id=x_peer(o), device_id_type=MESH)

    def gx_start(o, carry):
        gx(o).start()
        return carry

    def gx_wait(o, carry):
        gx(o).wait()
        return carry

    lax.fori_loop(1, nx, gx_start, 0)
    lax.fori_loop(1, nx, gx_wait, 0)

    def gz(side, s):
        block = (z - s + nz) % nz if side == 0 else (z + s) % nz
        return pltpu.make_async_remote_copy(
            src_ref=slab(block * nx, nx), dst_ref=slab(block * nx, nx),
            send_sem=gz_send.at[side, s], recv_sem=gz_recv.at[side, s],
            device_id=z_peer(1 if side == 0 else -1), device_id_type=MESH)

    d_blocks = n_d // L
    per = L // chunk

    def turn(b):
        block = pts[:, pl.ds(pl.multiple_of(b * L, L), L)].astype(F32)
        flipped = block.T.astype(BF16)
        for g in range(per):
            place = (g % nx) * nz + b * (per // nx) + g // nx
            pts_t[pl.ds(pl.multiple_of(place * chunk, chunk), chunk), :] = flipped[g * chunk:(g + 1) * chunk, :]

    gz(0, 0).start()
    gz(1, 0).start()
    load.wait()

    def ring(s, carry):
        gz(0, s).wait_recv()
        gz(0, s + 1).start()
        gz(1, s).wait_recv()

        @pl.when(s + 1 < left_steps)
        def _():
            gz(1, s + 1).start()
        return carry

    def turn_step(b, carry):
        turn(b)
        return carry

    lax.fori_loop(0, left_steps, ring, 0)
    lax.fori_loop(0, d_blocks, turn_step, 0)
    gz(0, right_steps - 1).wait_recv()

    def gz_drain(s, carry):
        gz(0, s).wait_send()

        @pl.when(s < left_steps)
        def _():
            gz(1, s).wait_send()
        return carry

    lax.fori_loop(0, right_steps, gz_drain, 0)

    top[...] = jnp.full(top.shape, -jnp.inf, F32)

    def logits(t, carry):
        where = pl.ds(pl.multiple_of(t * wide, wide), wide)
        part = piece[:, where]
        long = part.astype(F32)
        norms = jnp.sum(long * long, axis=0, keepdims=True)
        dots = jnp.dot(pts[...], part, preferred_element_type=F32)
        score = (2.0 * dots - norms) * 1.25
        mass[:, where] = score
        best = score[:, :L]
        for i in range(1, wide // L):
            best = jnp.maximum(best, score[:, i * L:(i + 1) * L])
        top[...] = jnp.maximum(top[...], best)
        return carry

    lax.fori_loop(0, n_k // wide, logits, 0)

    def swap(buf, slot, n, me, peer, send, recv):
        def copy(o):
            return pltpu.make_async_remote_copy(
                src_ref=buf.at[me], dst_ref=buf.at[me], send_sem=send.at[slot, o],
                recv_sem=recv.at[slot, o], device_id=peer(o), device_id_type=MESH)

        def start(o, carry):
            copy(o).start()
            return carry

        def wait(o, carry):
            copy(o).wait()
            return carry

        return (lambda: lax.fori_loop(1, n, start, 0)), (lambda: lax.fori_loop(1, n, wait, 0))

    def total(buf, n):
        out = buf[0]
        for i in range(1, n):
            out = out + buf[i]
        return out

    def row_block(j):
        return pl.ds(pl.multiple_of(j * L, L), L)

    def weigh(j, carry):
        block = top[row_block(j), :]
        peak = jnp.max(block, axis=1, keepdims=True)
        soft[c, pl.ds(j, 1), :] = jnp.max(block.T, axis=0, keepdims=True)
        acc = jnp.zeros((L, L), F32)
        for t in range(col_tiles):
            w = jnp.exp(mass[row_block(j), t * L:(t + 1) * L] - peak)
            mass[row_block(j), t * L:(t + 1) * L] = w
            acc = acc + w
        soft[c, pl.ds(row_blocks + j, 1), :] = jnp.sum(acc.T, axis=0, keepdims=True)
        return carry

    lax.fori_loop(0, row_blocks, weigh, 0)
    start, wait = swap(soft, 0, nc, c, cen_peer, soft_send, soft_recv)
    start()
    wait()
    peaks = soft[0, :row_blocks]
    for i in range(1, nc):
        peaks = jnp.maximum(peaks, soft[i, :row_blocks])
    sums = jnp.zeros_like(peaks)
    for i in range(nc):
        sums = sums + soft[i, row_blocks:] * jnp.exp(soft[i, :row_blocks] - peaks)
    scale_rows = jnp.exp(soft[c, :row_blocks] - peaks) / sums

    def spread(scales, j):
        return jnp.broadcast_to(scales[j:j + 1, :], (L, L)).T

    def add_down(v):
        return jnp.sum(v, axis=0, keepdims=True)

    def reduce_cols(slot):
        start_a, wait_a = swap(cols_a.at[slot], slot, na, ga, a_peer, ca_send, ca_recv)
        start_b, wait_b = swap(cols_b.at[slot], slot, zb, gb, b_peer, cb_send, cb_recv)

        def middle():
            wait_a()
            cols_b[slot, gb] = total(cols_a.at[slot], na)
            start_b()

        def last():
            wait_b()
            return total(cols_b.at[slot], zb)

        return start_a, middle, last

    for turn_no in range(PASSES):
        acc = [jnp.zeros((1, L), F32) for _ in range(col_tiles)]
        for j in range(row_blocks):
            scale = spread(scale_rows, j)
            for t in range(col_tiles):
                m = mass[j * L:(j + 1) * L, t * L:(t + 1) * L] * scale
                mass[j * L:(j + 1) * L, t * L:(t + 1) * L] = m
                acc[t] = acc[t] + add_down(m)
        for t in range(col_tiles):
            cols_a[turn_no, ga, t:t + 1, :] = acc[t]
        first, middle, last = reduce_cols(turn_no)
        first()
        middle()
        scale_cols = 1.0 / last()
        for j in range(row_blocks):
            acc_r = jnp.zeros((L, L), F32)
            for t in range(col_tiles):
                m = mass[j * L:(j + 1) * L, t * L:(t + 1) * L] * scale_cols[t:t + 1, :]
                mass[j * L:(j + 1) * L, t * L:(t + 1) * L] = m
                acc_r = acc_r + m
            rows[turn_no, c, j:j + 1, :] = add_down(acc_r.T)
        start, wait = swap(rows.at[turn_no], turn_no, nc, c, cen_peer, row_send, row_recv)
        start()
        wait()
        scale_rows = 1.0 / total(rows.at[turn_no], nc)

    acc = [jnp.zeros((1, L), F32) for _ in range(col_tiles)]
    for j in range(row_blocks):
        scale = spread(scale_rows, j)
        for t in range(col_tiles):
            m = (mass[j * L:(j + 1) * L, t * L:(t + 1) * L] * scale).astype(BF16)
            assign[j * L:(j + 1) * L, t * L:(t + 1) * L] = m
            acc[t] = acc[t] + add_down(m.astype(F32))
    store = pltpu.make_async_copy(assign, assign_ref, local_sem.at[1])
    store.start()
    for t in range(col_tiles):
        cols_a[PASSES, ga, t:t + 1, :] = acc[t]
    first, middle, last = reduce_cols(PASSES)
    first()

    half = n_d // nx

    def rx(o):
        return pltpu.make_async_remote_copy(
            src_ref=xsend.at[o - 1], dst_ref=xrecv.at[o - 1], send_sem=rx_send.at[o], recv_sem=rx_recv.at[o],
            device_id=x_peer(o), device_id_type=MESH)

    order = sorted(range(1, nx), key=lambda o: -min(o, nx - o)) + [0]
    for o in order:
        to = (x + o) % nx
        lhs_rows = pl.ds(pl.multiple_of(to * half, half), half)

        def product(t, carry):
            where = pl.ds(pl.multiple_of(t * wide, wide), wide)
            part = jnp.dot(pts_t[lhs_rows, :], assign[:, where], preferred_element_type=F32)
            if o:
                xsend[o - 1, :, where] = part.astype(BF16)
            else:
                own[:, where] = part
            return carry

        lax.fori_loop(0, n_k // wide, product, 0)
        if o:
            rx(o).start()
    middle()

    for o in range(1, nx):
        rx(o).wait_recv()

    def gather_up(i, carry):
        here = pl.ds(pl.multiple_of(i * chunk, chunk), chunk)
        v = own[here, :]
        for o in range(1, nx):
            v = v + xrecv[o - 1, here, :].astype(F32)
        own[here, :] = v
        return carry

    lax.fori_loop(0, nz, gather_up, 0)

    def share(b):
        return own[pl.ds(pl.multiple_of(b * chunk, chunk), chunk), :]

    def rz(side, s):
        return pltpu.make_async_remote_copy(
            src_ref=zsend.at[side, s], dst_ref=zrecv.at[side, s],
            send_sem=rz_send.at[side, s], recv_sem=rz_recv.at[side, s],
            device_id=z_peer(1 if side == 0 else -1), device_id_type=MESH)

    zsend[0, 0] = share((z + right_steps) % nz)
    rz(0, 0).start()
    zsend[1, 0] = share((z + nz - left_steps) % nz)
    rz(1, 0).start()

    def ring_sum(s, carry):
        rz(0, s - 1).wait_recv()
        zsend[0, s] = zrecv[0, s - 1] + share((z + right_steps - s) % nz)
        rz(0, s).start()
        rz(1, s - 1).wait_recv()

        @pl.when(s < left_steps)
        def _():
            zsend[1, s] = zrecv[1, s - 1] + share((z + nz - left_steps + s) % nz)
            rz(1, s).start()
        return carry

    lax.fori_loop(1, right_steps, ring_sum, 0)
    counts = last()
    rz(0, right_steps - 1).wait_recv()
    numer = share(z) + zrecv[0, right_steps - 1] + zrecv[1, left_steps - 1]
    for t in range(col_tiles):
        newc_ref[:, t * L:(t + 1) * L] = numer[:, t * L:(t + 1) * L] / counts[t:t + 1, :]

    def rz_drain(s, carry):
        rz(0, s).wait_send()

        @pl.when(s < left_steps)
        def _():
            rz(1, s).wait_send()
        return carry

    lax.fori_loop(0, right_steps, rz_drain, 0)
    for o in range(1, nx):
        rx(o).wait_send()
    store.wait()


def on_device(nx, nz, nc, za, points, centroids_t):
    n_rows, n_d = points.shape
    chunk, n_k = centroids_t.shape
    na, zb = za * nx, nz // za
    rb, ct = n_rows // L, n_k // L
    assert nz // 2 == nz - 1 - nz // 2 + 1
    right = nz // 2
    vmem = pltpu.VMEM
    dma = pltpu.SemaphoreType.DMA
    return pl.pallas_call(
        functools.partial(kernel, nx, nz, nc, za),
        out_shape=(
            jax.ShapeDtypeStruct((chunk, n_k), F32),
            jax.ShapeDtypeStruct((n_rows, n_k), BF16),
        ),
        in_specs=[pl.BlockSpec(memory_space=pl.ANY), pl.BlockSpec(memory_space=vmem)],
        out_specs=(pl.BlockSpec(memory_space=vmem), pl.BlockSpec(memory_space=pl.ANY)),
        scratch_shapes=[
            vmem((n_rows, n_d), BF16),
            vmem((n_d, n_rows), BF16),
            vmem((n_d, n_k), BF16),
            vmem((n_rows, n_k), F32),
            vmem((n_rows, L), F32),
            vmem((n_rows, n_k), BF16),
            vmem((n_d // nx, n_k), F32),
            vmem((nx - 1, n_d // nx, n_k), BF16),
            vmem((nx - 1, n_d // nx, n_k), BF16),
            vmem((2, right, chunk, n_k), F32),
            vmem((2, right, chunk, n_k), F32),
            vmem((nc, 2 * rb, L), F32),
            vmem((PASSES, nc, rb, L), F32),
            vmem((PASSES + 1, na, ct, L), F32),
            vmem((PASSES + 1, zb, ct, L), F32),
            dma((2,)),
            dma((nx,)), dma((nx,)),
            dma((2, right)), dma((2, right)),
            dma((1, nc)), dma((1, nc)),
            dma((PASSES, nc)), dma((PASSES, nc)),
            dma((PASSES + 1, na)), dma((PASSES + 1, na)),
            dma((PASSES + 1, zb)), dma((PASSES + 1, zb)),
            dma((nx,)), dma((nx,)),
            dma((2, right)), dma((2, right)),
        ],
        compiler_params=pltpu.CompilerParams(
            collective_id=0, has_side_effects=True, vmem_limit_bytes=50 * 1024 * 1024
        ),
    )(points, centroids_t)


def solution(mesh, nx=X_CHIPS, za=Z_GROUP):
    nz = mesh.shape["pts"] // nx
    return jax.shard_map(
        functools.partial(on_device, nx, nz, mesh.shape["cen"], za),
        mesh=mesh,
        in_specs=(P("pts", None), P("pts", "cen")),
        out_specs=(P("pts", "cen"), P("pts", "cen")),
        check_vma=False,
    )
```

time: 1390 us -> 173 us (0.12)
  the two profiles are of different devices: /device:TPU:8 before, /device:TPU:32 now
where the time goes in v1:
time: 173 us; the launch traced here: 172 us
  Pallas kernels  169 us (98%)
  local copies, waits for them, and re-layouts  2.7 us (2%)
    pallas_call x1, Pallas kernels, on_device(): pl.pallas_call(functools.partial(kernel, nx, nz, nc, za), out_shape=(jax....  169 us

profile of v1, /device:TPU:32, one launch (start us, length us, event | category | flops | bytes accessed | tf_op | source)
XLA Modules:
  0.0 172.4 jit_solution(16731040636673154205)
XLA Ops:
  0.6 0.0 copy-start
  0.6 0.7 copy-done
  1.4 169.1 %shard_map.41 = (f32[16,1024]{1,0:T(8,128)S(1)}, bf16[1024,1024]{1,0:T(8,128)(2,1)S(1)}) custom-call(bf16[1024,1024]{1,0:T(8,128)(2,1)} %points_ref.1, bf16[16,1024]{1,0:T(8,128)(2,1)S(1)} %copy-done), custom_call_target="tpu_custom_call" | custom-call | tf_op jit(solution)/shard_map/pallas_call | solution.py:369
  170.5 0.6 copy.6
  171.1 1.3 copy.7
Async XLA Ops:
  0.6 0.8 copy-start

commit v2 on v1

--- a/solution.py
+++ b/solution.py
@@ -17,7 +17,7 @@
 
 
 def kernel(nx, nz, nc, za, points_ref, cent_ref, newc_ref, assign_ref,
-           pts, pts_t, piece, mass, top, assign, own, xsend, xrecv, zsend, zrecv,
+           pts, pts_t, piece, mass, norms, top, assign, own, xsend, xrecv, zsend, zrecv,
            soft, rows, cols_a, cols_b,
            local_sem, gx_send, gx_recv, gz_send, gz_recv, soft_send, soft_recv,
            row_send, row_recv, ca_send, ca_recv, cb_send, cb_recv,
@@ -67,11 +67,10 @@
         lax.fori_loop(1, n, body, 0)
 
     greet(cen_peer, nc)
-    greet(a_peer, na)
-    greet(b_peer, zb)
+    greet(x_peer, nx)
     pl.semaphore_signal(barrier, inc=1, device_id=z_peer(1), device_id_type=MESH)
     pl.semaphore_signal(barrier, inc=1, device_id=z_peer(-1), device_id_type=MESH)
-    pl.semaphore_wait(barrier, (nc - 1) + (na - 1) + (zb - 1) + 2)
+    pl.semaphore_wait(barrier, (nc - 1) + (nx - 1) + 2)
 
     def slab(first, n):
         return piece.at[pl.ds(pl.multiple_of(first * chunk, chunk), n * chunk), :]
@@ -83,23 +82,23 @@
             src_ref=slab(p, 1), dst_ref=slab(p, 1), send_sem=gx_send.at[o], recv_sem=gx_recv.at[o],
             device_id=x_peer(o), device_id_type=MESH)
 
-    def gx_start(o, carry):
+    for o in range(1, nx):
         gx(o).start()
-        return carry
-
-    def gx_wait(o, carry):
-        gx(o).wait()
-        return carry
-
-    lax.fori_loop(1, nx, gx_start, 0)
-    lax.fori_loop(1, nx, gx_wait, 0)
-
-    def gz(side, s):
+
+    def gz(side, s, o):
         block = (z - s + nz) % nz if side == 0 else (z + s) % nz
+        part = slab(block * nx + (x - o + nx) % nx, 1)
         return pltpu.make_async_remote_copy(
-            src_ref=slab(block * nx, nx), dst_ref=slab(block * nx, nx),
-            send_sem=gz_send.at[side, s], recv_sem=gz_recv.at[side, s],
+            src_ref=part, dst_ref=part,
+            send_sem=gz_send.at[side, s, o], recv_sem=gz_recv.at[side, s, o],
             device_id=z_peer(1 if side == 0 else -1), device_id_type=MESH)
+
+    near = sorted(range(nx), key=lambda o: min(o, nx - o))
+    for o in near:
+        if o:
+            gx(o).wait_recv()
+        gz(0, 0, o).start()
+        gz(1, 0, o).start()
 
     d_blocks = n_d // L
     per = L // chunk
@@ -111,47 +110,67 @@
             place = (g % nx) * nz + b * (per // nx) + g // nx
             pts_t[pl.ds(pl.multiple_of(place * chunk, chunk), chunk), :] = flipped[g * chunk:(g + 1) * chunk, :]
 
-    gz(0, 0).start()
-    gz(1, 0).start()
     load.wait()
+    for b in range(left_steps, d_blocks):
+        turn(b)
 
     def ring(s, carry):
-        gz(0, s).wait_recv()
-        gz(0, s + 1).start()
-        gz(1, s).wait_recv()
-
-        @pl.when(s + 1 < left_steps)
+        for o in near:
+            gz(0, s, o).wait_recv()
+            gz(0, s + 1, o).start()
+            gz(1, s, o).wait_recv()
+
+            @pl.when(s + 1 < left_steps)
+            def _():
+                gz(1, s + 1, o).start()
+
+        @pl.when(s < d_blocks)
         def _():
-            gz(1, s + 1).start()
-        return carry
-
-    def turn_step(b, carry):
-        turn(b)
-        return carry
-
-    lax.fori_loop(0, left_steps, ring, 0)
-    lax.fori_loop(0, d_blocks, turn_step, 0)
-    gz(0, right_steps - 1).wait_recv()
-
-    def gz_drain(s, carry):
-        gz(0, s).wait_send()
-
-        @pl.when(s < left_steps)
-        def _():
-            gz(1, s).wait_send()
-        return carry
-
-    lax.fori_loop(0, right_steps, gz_drain, 0)
-
+            turn(s)
+        return carry
+
+    quarter = n_d // 4
+    mine = z // (nz // 4)
+
+    def depth(g):
+        return pl.ds(pl.multiple_of(g * quarter, quarter), quarter)
+
+    def dots_of(g, where):
+        part = piece[depth(g), where]
+        long = part.astype(F32)
+        dots = jnp.dot(pts[:, depth(g)], part, preferred_element_type=F32)
+        return dots, jnp.sum(long * long, axis=0, keepdims=True)
+
+    def first_dots(t, carry):
+        where = pl.ds(pl.multiple_of(t * wide, wide), wide)
+        dots, squares = dots_of(mine, where)
+        mass[:, where] = dots
+        norms[:, where] = squares
+        return carry
+
+    def more_dots(g):
+        def body(t, carry):
+            where = pl.ds(pl.multiple_of(t * wide, wide), wide)
+            dots, squares = dots_of(g, where)
+            mass[:, where] += dots
+            norms[:, where] += squares
+            return carry
+        return body
+
+    tiles = n_k // wide
+    lax.fori_loop(0, nz // 4, ring, 0)
+    lax.fori_loop(0, tiles, first_dots, 0)
+    lax.fori_loop(nz // 4, left_steps, ring, 0)
+    lax.fori_loop(0, tiles, more_dots((mine + 1) % 4), 0)
+    lax.fori_loop(0, tiles, more_dots((mine + 3) % 4), 0)
+    for o in near:
+        gz(0, right_steps - 1, o).wait_recv()
     top[...] = jnp.full(top.shape, -jnp.inf, F32)
 
     def logits(t, carry):
         where = pl.ds(pl.multiple_of(t * wide, wide), wide)
-        part = piece[:, where]
-        long = part.astype(F32)
-        norms = jnp.sum(long * long, axis=0, keepdims=True)
-        dots = jnp.dot(pts[...], part, preferred_element_type=F32)
-        score = (2.0 * dots - norms) * 1.25
+        dots, squares = dots_of((mine + 2) % 4, where)
+        score = (2.0 * (mass[:, where] + dots) - (norms[:, where] + squares)) * 1.25
         mass[:, where] = score
         best = score[:, :L]
         for i in range(1, wide // L):
@@ -159,7 +178,20 @@
         top[...] = jnp.maximum(top[...], best)
         return carry
 
-    lax.fori_loop(0, n_k // wide, logits, 0)
+    lax.fori_loop(0, tiles, logits, 0)
+
+    def gz_drain(s, carry):
+        for o in range(nx):
+            gz(0, s, o).wait_send()
+
+            @pl.when(s < left_steps)
+            def _():
+                gz(1, s, o).wait_send()
+        return carry
+
+    lax.fori_loop(0, right_steps, gz_drain, 0)
+    for o in range(1, nx):
+        gx(o).wait_send()
 
     def swap(buf, slot, n, me, peer, send, recv):
         def copy(o):
@@ -379,6 +411,7 @@
             vmem((n_d, n_rows), BF16),
             vmem((n_d, n_k), BF16),
             vmem((n_rows, n_k), F32),
+            vmem((1, n_k), F32),
             vmem((n_rows, L), F32),
             vmem((n_rows, n_k), BF16),
             vmem((n_d // nx, n_k), F32),
@@ -392,7 +425,7 @@
             vmem((PASSES + 1, zb, ct, L), F32),
             dma((2,)),
             dma((nx,)), dma((nx,)),
-            dma((2, right)), dma((2, right)),
+            dma((2, right, nx)), dma((2, right, nx)),
             dma((1, nc)), dma((1, nc)),
             dma((PASSES, nc)), dma((PASSES, nc)),
             dma((PASSES + 1, na)), dma((PASSES + 1, na)),

time: 173 us -> 160 us (0.925)
  the two profiles are of different devices: /device:TPU:32 before, /device:TPU:2 now
where the time goes in v2:
time: 160 us
  Pallas kernels  157 us (98%)
  local copies, waits for them, and re-layouts  2.7 us (2%)
    pallas_call x1, Pallas kernels, on_device(): pl.pallas_call(functools.partial(kernel, nx, nz, nc, za), out_shape=(jax....  157 us

profile of v2, /device:TPU:2, one launch (start us, length us, event | category | flops | bytes accessed | tf_op | source)
XLA Modules:
  0.0 160.2 jit_solution(13765503229232469389)
XLA Ops:
  0.6 0.0 copy-start
  0.6 0.7 copy-done
  1.4 156.8 %shard_map.41 = (f32[16,1024]{1,0:T(8,128)S(1)}, bf16[1024,1024]{1,0:T(8,128)(2,1)S(1)}) custom-call(bf16[1024,1024]{1,0:T(8,128)(2,1)} %points_ref.1, bf16[16,1024]{1,0:T(8,128)(2,1)S(1)} %copy-done), custom_call_target="tpu_custom_call" | custom-call | tf_op jit(solution)/shard_map/pallas_call | solution.py:401
  158.2 0.6 copy.6
  158.8 1.3 copy.7
Async XLA Ops:
  0.6 0.8 copy-start

commit v3 on v2

--- a/solution.py
+++ b/solution.py
@@ -14,10 +14,15 @@
 BF16 = jnp.bfloat16
 X_CHIPS = 4
 Z_GROUP = 2
+VIA = {1: 1, -1: -1, 2: -1, 4: 1, 5: -1, 7: 1, 8: 2, -2: 1, -4: -1, -5: 1, -7: -1}
+FEEDS = {3: (4, 2), 6: (7, 5, 8), -3: (-4, -2), -6: (-7, -5)}
+FAR = (6, -6, 3, -3)
+GREET_Z = (1, -1, 2, -2, 3, -3, 6, -6)
+PARTS = ((5, 4), (-7, 3), (2, 3), (-4, 3), (-1, 3))
 
 
 def kernel(nx, nz, nc, za, points_ref, cent_ref, newc_ref, assign_ref,
-           pts, pts_t, piece, mass, norms, top, assign, own, xsend, xrecv, zsend, zrecv,
+           pts, pts_t, piece, mass, norms, top, assign, own, prod, xsend, xrecv, zrecv,
            soft, rows, cols_a, cols_b,
            local_sem, gx_send, gx_recv, gz_send, gz_recv, soft_send, soft_recv,
            row_send, row_recv, ca_send, ca_recv, cb_send, cb_recv,
@@ -29,8 +34,6 @@
     wide = min(256, n_k)
     zb = nz // za
     na = za * nx
-    right_steps = nz // 2
-    left_steps = nz - 1 - right_steps
 
     p = lax.axis_index("pts")
     c = lax.axis_index("cen")
@@ -68,66 +71,114 @@
 
     greet(cen_peer, nc)
     greet(x_peer, nx)
-    pl.semaphore_signal(barrier, inc=1, device_id=z_peer(1), device_id_type=MESH)
-    pl.semaphore_signal(barrier, inc=1, device_id=z_peer(-1), device_id_type=MESH)
-    pl.semaphore_wait(barrier, (nc - 1) + (nx - 1) + 2)
-
-    def slab(first, n):
-        return piece.at[pl.ds(pl.multiple_of(first * chunk, chunk), n * chunk), :]
+    for e in GREET_Z:
+        pl.semaphore_signal(barrier, inc=1, device_id=z_peer(e), device_id_type=MESH)
+    pl.semaphore_wait(barrier, (nc - 1) + (nx - 1) + len(GREET_Z))
+
+    def slab(e, side):
+        first = ((z + nz + e) % nz) * nx + (x + nx + side) % nx
+        return piece.at[pl.ds(pl.multiple_of(first * chunk, chunk), chunk), :]
 
     piece[pl.ds(pl.multiple_of(p * chunk, chunk), chunk), :] = cent_ref[...]
 
-    def gx(o):
-        return pltpu.make_async_remote_copy(
-            src_ref=slab(p, 1), dst_ref=slab(p, 1), send_sem=gx_send.at[o], recv_sem=gx_recv.at[o],
-            device_id=x_peer(o), device_id_type=MESH)
-
-    for o in range(1, nx):
-        gx(o).start()
-
-    def gz(side, s, o):
-        block = (z - s + nz) % nz if side == 0 else (z + s) % nz
-        part = slab(block * nx + (x - o + nx) % nx, 1)
-        return pltpu.make_async_remote_copy(
-            src_ref=part, dst_ref=part,
-            send_sem=gz_send.at[side, s, o], recv_sem=gz_recv.at[side, s, o],
-            device_id=z_peer(1 if side == 0 else -1), device_id_type=MESH)
-
-    near = sorted(range(nx), key=lambda o: min(o, nx - o))
-    for o in near:
-        if o:
-            gx(o).wait_recv()
-        gz(0, 0, o).start()
-        gz(1, 0, o).start()
+    def gz(e, root):
+        at = root - e + 7
+        at = at + nz if at < 0 else at - nz if at >= nz else at
+        part = slab(root, 0)
+        return pltpu.make_async_remote_copy(
+            src_ref=part, dst_ref=part, send_sem=gz_send.at[at], recv_sem=gz_recv.at[at],
+            device_id=z_peer(e), device_id_type=MESH)
+
+    def gz_got(e):
+        part = slab(e, 0)
+        return pltpu.make_async_remote_copy(
+            src_ref=part, dst_ref=part, send_sem=gz_send.at[e + 7], recv_sem=gz_recv.at[e + 7],
+            device_id=z_peer(1), device_id_type=MESH)
+
+    def gx(e, frm, side):
+        part = slab(e, frm)
+        lane = 0 if frm == 0 and side == 1 else 1 if frm == 0 else 2
+        return pltpu.make_async_remote_copy(
+            src_ref=part, dst_ref=part, send_sem=gx_send.at[e + 7, lane], recv_sem=gx_recv.at[e + 7, lane],
+            device_id=x_peer(nx + side), device_id_type=MESH)
+
+    def gx_got(e, lane):
+        part = slab(e, (-1, 1, 2)[lane])
+        return pltpu.make_async_remote_copy(
+            src_ref=part, dst_ref=part, send_sem=gx_send.at[e + 7, lane], recv_sem=gx_recv.at[e + 7, lane],
+            device_id=x_peer(1), device_id_type=MESH)
+
+    sent_z = []
+    sent_x = []
+
+    def go_z(e, root):
+        gz(e, root).start()
+        sent_z.append((e, root))
+
+    def go_x(e, frm, side):
+        gx(e, frm, side).start()
+        sent_x.append((e, frm, side))
+
+    def x_near(e):
+        go_x(e, 0, 1)
+        go_x(e, 0, -1)
+
+    def x_on(e):
+        gx_got(e, 0).wait_recv()
+        gx_got(e, 1).wait_recv()
+        if e % 2 == 0:
+            go_x(e, -1, 1)
+        else:
+            go_x(e, 1, -1)
 
     d_blocks = n_d // L
-    per = L // chunk
 
     def turn(b):
         block = pts[:, pl.ds(pl.multiple_of(b * L, L), L)].astype(F32)
-        flipped = block.T.astype(BF16)
-        for g in range(per):
-            place = (g % nx) * nz + b * (per // nx) + g // nx
-            pts_t[pl.ds(pl.multiple_of(place * chunk, chunk), chunk), :] = flipped[g * chunk:(g + 1) * chunk, :]
-
+        pts_t[pl.ds(pl.multiple_of(b * L, L), L), :] = block.T.astype(BF16)
+
+    def turns(first, last):
+        def body(b, carry):
+            turn(b)
+            return carry
+        lax.fori_loop(first, last, body, 0)
+
+    for e in FAR + (1, -1):
+        go_z(e, 0)
+    x_near(0)
     load.wait()
-    for b in range(left_steps, d_blocks):
-        turn(b)
-
-    def ring(s, carry):
-        for o in near:
-            gz(0, s, o).wait_recv()
-            gz(0, s + 1, o).start()
-            gz(1, s, o).wait_recv()
-
-            @pl.when(s + 1 < left_steps)
-            def _():
-                gz(1, s + 1, o).start()
-
-        @pl.when(s < d_blocks)
-        def _():
-            turn(s)
-        return carry
+    turns(0, d_blocks // 2)
+    for e in (1, -1):
+        gz_got(e).wait_recv()
+        x_near(e)
+    for e in (3, -3):
+        gz_got(e).wait_recv()
+        go_z(1, e)
+        go_z(-1, e)
+        x_near(e)
+    x_on(0)
+    for e in (6, -6):
+        gz_got(e).wait_recv()
+        go_z(1, e)
+        go_z(-1, e)
+        if e == -6:
+            go_z(2, e)
+        x_near(e)
+    for e in (1, -1, 3, -3):
+        x_on(e)
+    for e in (2, -2, 4, -4):
+        gz_got(e).wait_recv()
+        x_near(e)
+    x_on(6)
+    x_on(-6)
+    for e in (5, -5, 7, -7, 8):
+        gz_got(e).wait_recv()
+        x_near(e)
+    turns(d_blocks // 2, d_blocks)
+    ahead = 3 * nx * chunk
+    pts_t[n_d:n_d + ahead, :] = pts_t[:ahead, :]
+    for e in (2, -2, 4, -4, 5, -5, 7, -7, 8):
+        x_on(e)
 
     quarter = n_d // 4
     mine = z // (nz // 4)
@@ -158,13 +209,14 @@
         return body
 
     tiles = n_k // wide
-    lax.fori_loop(0, nz // 4, ring, 0)
+    for e in (0, 1, -1, 3, -3, 2, -2):
+        gx_got(e, 2).wait_recv()
     lax.fori_loop(0, tiles, first_dots, 0)
-    lax.fori_loop(nz // 4, left_steps, ring, 0)
+    for e in (6, -6, 4, -4, 5, -5, 7, -7):
+        gx_got(e, 2).wait_recv()
     lax.fori_loop(0, tiles, more_dots((mine + 1) % 4), 0)
     lax.fori_loop(0, tiles, more_dots((mine + 3) % 4), 0)
-    for o in near:
-        gz(0, right_steps - 1, o).wait_recv()
+    gx_got(8, 2).wait_recv()
     top[...] = jnp.full(top.shape, -jnp.inf, F32)
 
     def logits(t, carry):
@@ -180,18 +232,10 @@
 
     lax.fori_loop(0, tiles, logits, 0)
 
-    def gz_drain(s, carry):
-        for o in range(nx):
-            gz(0, s, o).wait_send()
-
-            @pl.when(s < left_steps)
-            def _():
-                gz(1, s, o).wait_send()
-        return carry
-
-    lax.fori_loop(0, right_steps, gz_drain, 0)
-    for o in range(1, nx):
-        gx(o).wait_send()
+    for e, root in sent_z:
+        gz(e, root).wait_send()
+    for e, frm, side in sent_x:
+        gx(e, frm, side).wait_send()
 
     def swap(buf, slot, n, me, peer, send, recv):
         def copy(o):
@@ -303,89 +347,74 @@
     first, middle, last = reduce_cols(PASSES)
     first()
 
-    half = n_d // nx
-
-    def rx(o):
-        return pltpu.make_async_remote_copy(
-            src_ref=xsend.at[o - 1], dst_ref=xrecv.at[o - 1], send_sem=rx_send.at[o], recv_sem=rx_recv.at[o],
+    def rx(first, n, o):
+        k = first + 7
+        return pltpu.make_async_remote_copy(
+            src_ref=xsend.at[pl.ds(k, n), (x + o) % nx], dst_ref=xrecv.at[o - 1, pl.ds(k, n)],
+            send_sem=rx_send.at[o - 1, k], recv_sem=rx_recv.at[o - 1, k],
             device_id=x_peer(o), device_id_type=MESH)
 
-    order = sorted(range(1, nx), key=lambda o: -min(o, nx - o)) + [0]
-    for o in order:
-        to = (x + o) % nx
-        lhs_rows = pl.ds(pl.multiple_of(to * half, half), half)
+    def rz(e):
+        return pltpu.make_async_remote_copy(
+            src_ref=own.at[e + 7], dst_ref=zrecv.at[e + 7], send_sem=rz_send.at[e + 7], recv_sem=rz_recv.at[e + 7],
+            device_id=z_peer(VIA.get(e, e)), device_id_type=MESH)
+
+    peers = sorted(range(1, nx), key=lambda o: -min(o, nx - o))
+    block = nx * chunk
+    for first, n in PARTS:
+        depth_rows = pl.ds(pl.multiple_of(((z + nz + first) % nz) * block, block), n * block)
+        k = first + 7
 
         def product(t, carry):
             where = pl.ds(pl.multiple_of(t * wide, wide), wide)
-            part = jnp.dot(pts_t[lhs_rows, :], assign[:, where], preferred_element_type=F32)
-            if o:
-                xsend[o - 1, :, where] = part.astype(BF16)
-            else:
-                own[:, where] = part
-            return carry
-
-        lax.fori_loop(0, n_k // wide, product, 0)
-        if o:
-            rx(o).start()
-    middle()
-
-    for o in range(1, nx):
-        rx(o).wait_recv()
-
-    def gather_up(i, carry):
-        here = pl.ds(pl.multiple_of(i * chunk, chunk), chunk)
-        v = own[here, :]
-        for o in range(1, nx):
-            v = v + xrecv[o - 1, here, :].astype(F32)
-        own[here, :] = v
-        return carry
-
-    lax.fori_loop(0, nz, gather_up, 0)
-
-    def share(b):
-        return own[pl.ds(pl.multiple_of(b * chunk, chunk), chunk), :]
-
-    def rz(side, s):
-        return pltpu.make_async_remote_copy(
-            src_ref=zsend.at[side, s], dst_ref=zrecv.at[side, s],
-            send_sem=rz_send.at[side, s], recv_sem=rz_recv.at[side, s],
-            device_id=z_peer(1 if side == 0 else -1), device_id_type=MESH)
-
-    zsend[0, 0] = share((z + right_steps) % nz)
-    rz(0, 0).start()
-    zsend[1, 0] = share((z + nz - left_steps) % nz)
-    rz(1, 0).start()
-
-    def ring_sum(s, carry):
-        rz(0, s - 1).wait_recv()
-        zsend[0, s] = zrecv[0, s - 1] + share((z + right_steps - s) % nz)
-        rz(0, s).start()
-        rz(1, s - 1).wait_recv()
-
-        @pl.when(s < left_steps)
-        def _():
-            zsend[1, s] = zrecv[1, s - 1] + share((z + nz - left_steps + s) % nz)
-            rz(1, s).start()
-        return carry
-
-    lax.fori_loop(1, right_steps, ring_sum, 0)
+            part = jnp.dot(pts_t[depth_rows, :], assign[:, where], preferred_element_type=F32)
+            part = part.reshape(n, nx, chunk, wide)
+            prod[k:k + n, :, :, where] = part
+            xsend[k:k + n, :, :, where] = part.astype(BF16)
+            return carry
+
+        lax.fori_loop(0, tiles, product, 0)
+        for o in peers:
+            rx(first, n, o).start()
+
+    def centre(e):
+        v = own[e + 7]
+        for f in FEEDS[e]:
+            rz(f).wait_recv()
+            v = v + zrecv[f + 7]
+        own[e + 7] = v
+        rz(e).start()
+
+    for i, (first, n) in enumerate(PARTS):
+        for o in peers:
+            rx(first, n, o).wait_recv()
+        for e in range(first, first + n):
+            v = prod[e + 7, x]
+            for o in range(1, nx):
+                v = v + xrecv[o - 1, e + 7].astype(F32)
+            own[e + 7] = v
+            if e in VIA:
+                rz(e).start()
+        if i:
+            before = PARTS[i - 1]
+            for e in FEEDS:
+                if before[0] <= e < before[0] + before[1]:
+                    centre(e)
+        else:
+            middle()
     counts = last()
-    rz(0, right_steps - 1).wait_recv()
-    numer = share(z) + zrecv[0, right_steps - 1] + zrecv[1, left_steps - 1]
+    numer = own[7]
+    for e in (1, -1) + FAR:
+        rz(e).wait_recv()
+        numer = numer + zrecv[e + 7]
     for t in range(col_tiles):
         newc_ref[:, t * L:(t + 1) * L] = numer[:, t * L:(t + 1) * L] / counts[t:t + 1, :]
-
-    def rz_drain(s, carry):
-        rz(0, s).wait_send()
-
-        @pl.when(s < left_steps)
-        def _():
-            rz(1, s).wait_send()
-        return carry
-
-    lax.fori_loop(0, right_steps, rz_drain, 0)
-    for o in range(1, nx):
-        rx(o).wait_send()
+    for e in range(-7, 9):
+        if e:
+            rz(e).wait_send()
+    for first, n in PARTS:
+        for o in peers:
+            rx(first, n, o).wait_send()
     store.wait()
 
 
@@ -394,8 +423,7 @@
     chunk, n_k = centroids_t.shape
     na, zb = za * nx, nz // za
     rb, ct = n_rows // L, n_k // L
-    assert nz // 2 == nz - 1 - nz // 2 + 1
-    right = nz // 2
+    assert nz == 16
     vmem = pltpu.VMEM
     dma = pltpu.SemaphoreType.DMA
     return pl.pallas_call(
@@ -408,30 +436,30 @@
         out_specs=(pl.BlockSpec(memory_space=vmem), pl.BlockSpec(memory_space=pl.ANY)),
         scratch_shapes=[
             vmem((n_rows, n_d), BF16),
-            vmem((n_d, n_rows), BF16),
+            vmem((n_d + 3 * nx * chunk, n_rows), BF16),
             vmem((n_d, n_k), BF16),
             vmem((n_rows, n_k), F32),
             vmem((1, n_k), F32),
             vmem((n_rows, L), F32),
             vmem((n_rows, n_k), BF16),
-            vmem((n_d // nx, n_k), F32),
-            vmem((nx - 1, n_d // nx, n_k), BF16),
-            vmem((nx - 1, n_d // nx, n_k), BF16),
-            vmem((2, right, chunk, n_k), F32),
-            vmem((2, right, chunk, n_k), F32),
+            vmem((nz, chunk, n_k), F32),
+            vmem((nz, nx, chunk, n_k), F32),
+            vmem((nz, nx, chunk, n_k), BF16),
+            vmem((nx - 1, nz, chunk, n_k), BF16),
+            vmem((nz, chunk, n_k), F32),
             vmem((nc, 2 * rb, L), F32),
             vmem((PASSES, nc, rb, L), F32),
             vmem((PASSES + 1, na, ct, L), F32),
             vmem((PASSES + 1, zb, ct, L), F32),
             dma((2,)),
-            dma((nx,)), dma((nx,)),
-            dma((2, right, nx)), dma((2, right, nx)),
+            dma((nz, 3)), dma((nz, 3)),
+            dma((nz,)), dma((nz,)),
             dma((1, nc)), dma((1, nc)),
             dma((PASSES, nc)), dma((PASSES, nc)),
             dma((PASSES + 1, na)), dma((PASSES + 1, na)),
             dma((PASSES + 1, zb)), dma((PASSES + 1, zb)),
-            dma((nx,)), dma((nx,)),
-            dma((2, right)), dma((2, right)),
+            dma((nx - 1, nz)), dma((nx - 1, nz)),
+            dma((nz,)), dma((nz,)),
         ],
         compiler_params=pltpu.CompilerParams(
             collective_id=0, has_side_effects=True, vmem_limit_bytes=50 * 1024 * 1024

time: 160 us -> 145 us (0.906)
  the two profiles are of different devices: /device:TPU:2 before, /device:TPU:46 now
where the time goes in v3:
time: 145 us; the launch traced here: 144 us
  Pallas kernels  141 us (97%)
  local copies, waits for them, and re-layouts  2.7 us (2%)
    pallas_call x1, Pallas kernels, on_device(): pl.pallas_call(functools.partial(kernel, nx, nz, nc, za), out_shape=(jax....  141 us

profile of v3, /device:TPU:46, one launch (start us, length us, event | category | flops | bytes accessed | tf_op | source)
XLA Modules:
  0.0 144.4 jit_solution(1794678468802228526)
XLA Ops:
  0.6 0.0 copy-start
  0.6 0.7 copy-done
  1.4 141.0 %shard_map.41 = (f32[16,1024]{1,0:T(8,128)S(1)}, bf16[1024,1024]{1,0:T(8,128)(2,1)S(1)}) custom-call(bf16[1024,1024]{1,0:T(8,128)(2,1)} %points_ref.1, bf16[16,1024]{1,0:T(8,128)(2,1)S(1)} %copy-done), custom_call_target="tpu_custom_call" | custom-call | tf_op jit(solution)/shard_map/pallas_call | solution.py:429
  142.4 0.6 copy.6
  143.1 1.3 copy.7
Async XLA Ops:
  0.6 0.8 copy-start

commit v4 on v3

--- a/solution.py
+++ b/solution.py
@@ -15,18 +15,19 @@
 X_CHIPS = 4
 Z_GROUP = 2
 VIA = {1: 1, -1: -1, 2: -1, 4: 1, 5: -1, 7: 1, 8: 2, -2: 1, -4: -1, -5: 1, -7: -1}
-FEEDS = {3: (4, 2), 6: (7, 5, 8), -3: (-4, -2), -6: (-7, -5)}
+FEEDS = {6: (7, 5, 8), -6: (-7, -5), 3: (4, 2, 6), -3: (-4, -2, -6)}
+STEP = {6: 3, -6: -3, 3: 3, -3: -3}
 FAR = (6, -6, 3, -3)
 GREET_Z = (1, -1, 2, -2, 3, -3, 6, -6)
 PARTS = ((5, 4), (-7, 3), (2, 3), (-4, 3), (-1, 3))
 
 
 def kernel(nx, nz, nc, za, points_ref, cent_ref, newc_ref, assign_ref,
-           pts, pts_t, piece, mass, norms, top, assign, own, prod, xsend, xrecv, zrecv,
+           pts, pts_t, piece, mass, norms, top, assign, own, prod, xfar, xfar_in, xsend, xrecv, zrecv,
            soft, rows, cols_a, cols_b,
            local_sem, gx_send, gx_recv, gz_send, gz_recv, soft_send, soft_recv,
            row_send, row_recv, ca_send, ca_recv, cb_send, cb_recv,
-           rx_send, rx_recv, rz_send, rz_recv):
+           rx1_send, rx1_recv, rx2_send, rx2_recv, rz_send, rz_recv):
     n_rows, n_d = points_ref.shape
     chunk, n_k = cent_ref.shape
     row_blocks = n_rows // L
@@ -177,7 +178,7 @@
     turns(d_blocks // 2, d_blocks)
     ahead = 3 * nx * chunk
     pts_t[n_d:n_d + ahead, :] = pts_t[:ahead, :]
-    for e in (2, -2, 4, -4, 5, -5, 7, -7, 8):
+    for e in (2, -2, 4, -4):
         x_on(e)
 
     quarter = n_d // 4
@@ -212,6 +213,8 @@
     for e in (0, 1, -1, 3, -3, 2, -2):
         gx_got(e, 2).wait_recv()
     lax.fori_loop(0, tiles, first_dots, 0)
+    for e in (5, -5, 7, -7, 8):
+        x_on(e)
     for e in (6, -6, 4, -4, 5, -5, 7, -7):
         gx_got(e, 2).wait_recv()
     lax.fori_loop(0, tiles, more_dots((mine + 1) % 4), 0)
@@ -347,19 +350,27 @@
     first, middle, last = reduce_cols(PASSES)
     first()
 
-    def rx(first, n, o):
+    half = n_k // 2
+
+    def rx1(first, n, side):
         k = first + 7
         return pltpu.make_async_remote_copy(
-            src_ref=xsend.at[pl.ds(k, n), (x + o) % nx], dst_ref=xrecv.at[o - 1, pl.ds(k, n)],
-            send_sem=rx_send.at[o - 1, k], recv_sem=rx_recv.at[o - 1, k],
-            device_id=x_peer(o), device_id_type=MESH)
+            src_ref=xfar.at[side, pl.ds(k, n)], dst_ref=xfar_in.at[side, pl.ds(k, n)],
+            send_sem=rx1_send.at[side, k], recv_sem=rx1_recv.at[side, k],
+            device_id=x_peer(1 if side == 0 else nx - 1), device_id_type=MESH)
+
+    def rx2(first, n, side):
+        k = first + 7
+        return pltpu.make_async_remote_copy(
+            src_ref=xsend.at[side, pl.ds(k, n)], dst_ref=xrecv.at[side, pl.ds(k, n)],
+            send_sem=rx2_send.at[side, k], recv_sem=rx2_recv.at[side, k],
+            device_id=x_peer(1 if side == 0 else nx - 1), device_id_type=MESH)
 
     def rz(e):
         return pltpu.make_async_remote_copy(
             src_ref=own.at[e + 7], dst_ref=zrecv.at[e + 7], send_sem=rz_send.at[e + 7], recv_sem=rz_recv.at[e + 7],
-            device_id=z_peer(VIA.get(e, e)), device_id_type=MESH)
-
-    peers = sorted(range(1, nx), key=lambda o: -min(o, nx - o))
+            device_id=z_peer(VIA[e] if e in VIA else STEP[e]), device_id_type=MESH)
+
     block = nx * chunk
     for first, n in PARTS:
         depth_rows = pl.ds(pl.multiple_of(((z + nz + first) % nz) * block, block), n * block)
@@ -368,14 +379,31 @@
         def product(t, carry):
             where = pl.ds(pl.multiple_of(t * wide, wide), wide)
             part = jnp.dot(pts_t[depth_rows, :], assign[:, where], preferred_element_type=F32)
-            part = part.reshape(n, nx, chunk, wide)
-            prod[k:k + n, :, :, where] = part
-            xsend[k:k + n, :, :, where] = part.astype(BF16)
+            prod[k:k + n, :, :, where] = part.reshape(n, nx, chunk, wide)
             return carry
 
         lax.fori_loop(0, tiles, product, 0)
-        for o in peers:
-            rx(first, n, o).start()
+        for e in range(first, first + n):
+            far = prod[e + 7, (x + 2) % nx].astype(BF16)
+            xfar[0, e + 7] = far[:, :half]
+            xfar[1, e + 7] = far[:, half:]
+        for side in range(2):
+            rx1(first, n, side).start()
+
+    def forward(first, n):
+        for side in range(2):
+            rx1(first, n, side).wait_recv()
+        for side in range(2):
+            for e in range(first, first + n):
+                v = prod[e + 7, (x + 1 + 2 * side) % nx]
+                w = xfar_in[side, e + 7].astype(F32)
+                if side == 0:
+                    xsend[side, e + 7, :, :half] = (v[:, :half] + w).astype(BF16)
+                    xsend[side, e + 7, :, half:] = v[:, half:].astype(BF16)
+                else:
+                    xsend[side, e + 7, :, :half] = v[:, :half].astype(BF16)
+                    xsend[side, e + 7, :, half:] = (v[:, half:] + w).astype(BF16)
+            rx2(first, n, side).start()
 
     def centre(e):
         v = own[e + 7]
@@ -385,16 +413,17 @@
         own[e + 7] = v
         rz(e).start()
 
+    forward(*PARTS[0])
+    forward(*PARTS[1])
     for i, (first, n) in enumerate(PARTS):
-        for o in peers:
-            rx(first, n, o).wait_recv()
+        for side in range(2):
+            rx2(first, n, side).wait_recv()
         for e in range(first, first + n):
-            v = prod[e + 7, x]
-            for o in range(1, nx):
-                v = v + xrecv[o - 1, e + 7].astype(F32)
-            own[e + 7] = v
+            own[e + 7] = prod[e + 7, x] + xrecv[0, e + 7].astype(F32) + xrecv[1, e + 7].astype(F32)
             if e in VIA:
                 rz(e).start()
+        if i + 2 < len(PARTS):
+            forward(*PARTS[i + 2])
         if i:
             before = PARTS[i - 1]
             for e in FEEDS:
@@ -404,7 +433,7 @@
             middle()
     counts = last()
     numer = own[7]
-    for e in (1, -1) + FAR:
+    for e in (1, -1, 3, -3):
         rz(e).wait_recv()
         numer = numer + zrecv[e + 7]
     for t in range(col_tiles):
@@ -413,8 +442,9 @@
         if e:
             rz(e).wait_send()
     for first, n in PARTS:
-        for o in peers:
-            rx(first, n, o).wait_send()
+        for side in range(2):
+            rx1(first, n, side).wait_send()
+            rx2(first, n, side).wait_send()
     store.wait()
 
 
@@ -423,7 +453,7 @@
     chunk, n_k = centroids_t.shape
     na, zb = za * nx, nz // za
     rb, ct = n_rows // L, n_k // L
-    assert nz == 16
+    assert nz == 16 and nx == 4
     vmem = pltpu.VMEM
     dma = pltpu.SemaphoreType.DMA
     return pl.pallas_call(
@@ -444,8 +474,10 @@
             vmem((n_rows, n_k), BF16),
             vmem((nz, chunk, n_k), F32),
             vmem((nz, nx, chunk, n_k), F32),
-            vmem((nz, nx, chunk, n_k), BF16),
-            vmem((nx - 1, nz, chunk, n_k), BF16),
+            vmem((2, nz, chunk, n_k // 2), BF16),
+            vmem((2, nz, chunk, n_k // 2), BF16),
+            vmem((2, nz, chunk, n_k), BF16),
+            vmem((2, nz, chunk, n_k), BF16),
             vmem((nz, chunk, n_k), F32),
             vmem((nc, 2 * rb, L), F32),
             vmem((PASSES, nc, rb, L), F32),
@@ -458,7 +490,8 @@
             dma((PASSES, nc)), dma((PASSES, nc)),
             dma((PASSES + 1, na)), dma((PASSES + 1, na)),
             dma((PASSES + 1, zb)), dma((PASSES + 1, zb)),
-            dma((nx - 1, nz)), dma((nx - 1, nz)),
+            dma((2, nz)), dma((2, nz)),
+            dma((2, nz)), dma((2, nz)),
             dma((nz,)), dma((nz,)),
         ],
         compiler_params=pltpu.CompilerParams(

time: 145 us -> 146 us (level)
  the two profiles are of different devices: /device:TPU:46 before, /device:TPU:32 now
where the time goes in v4:
time: 146 us
  Pallas kernels  143 us (98%)
  local copies, waits for them, and re-layouts  2.7 us (2%)
    pallas_call x1, Pallas kernels, on_device(): pl.pallas_call(functools.partial(kernel, nx, nz, nc, za), out_shape=(jax....  143 us

profile of v4, /device:TPU:32, one launch (start us, length us, event | category | flops | bytes accessed | tf_op | source)
XLA Modules:
  0.0 146.0 jit_solution(17004511117749485590)
XLA Ops:
  0.6 0.0 copy-start
  0.6 0.7 copy-done
  1.4 142.7 %shard_map.41 = (f32[16,1024]{1,0:T(8,128)S(1)}, bf16[1024,1024]{1,0:T(8,128)(2,1)S(1)}) custom-call(bf16[1024,1024]{1,0:T(8,128)(2,1)} %points_ref.1, bf16[16,1024]{1,0:T(8,128)(2,1)S(1)} %copy-done), custom_call_target="tpu_custom_call" | custom-call | tf_op jit(solution)/shard_map/pallas_call | solution.py:459
  144.0 0.6 copy.6
  144.7 1.3 copy.7
Async XLA Ops:
  0.6 0.8 copy-start

commit v5 on v4

--- a/solution.py
+++ b/solution.py
@@ -13,16 +13,15 @@
 F32 = jnp.float32
 BF16 = jnp.bfloat16
 X_CHIPS = 4
-Z_GROUP = 2
 VIA = {1: 1, -1: -1, 2: -1, 4: 1, 5: -1, 7: 1, 8: 2, -2: 1, -4: -1, -5: 1, -7: -1}
 FEEDS = {6: (7, 5, 8), -6: (-7, -5), 3: (4, 2, 6), -3: (-4, -2, -6)}
 STEP = {6: 3, -6: -3, 3: 3, -3: -3}
-FAR = (6, -6, 3, -3)
-GREET_Z = (1, -1, 2, -2, 3, -3, 6, -6)
+GREET_Z = (1, -1, 2, -2, 3, -3)
+CENTRES = (6, -6, 3, -3)
 PARTS = ((5, 4), (-7, 3), (2, 3), (-4, 3), (-1, 3))
 
 
-def kernel(nx, nz, nc, za, points_ref, cent_ref, newc_ref, assign_ref,
+def kernel(nx, nz, nc, points_ref, cent_ref, newc_ref, assign_ref,
            pts, pts_t, piece, mass, norms, top, assign, own, prod, xfar, xfar_in, xsend, xrecv, zrecv,
            soft, rows, cols_a, cols_b,
            local_sem, gx_send, gx_recv, gz_send, gz_recv, soft_send, soft_recv,
@@ -33,25 +32,14 @@
     row_blocks = n_rows // L
     col_tiles = n_k // L
     wide = min(256, n_k)
-    zb = nz // za
-    na = za * nx
 
     p = lax.axis_index("pts")
     c = lax.axis_index("cen")
     z = p // nx
     x = p % nx
-    ga = (z % za) * nx + x
-    gb = z // za
 
     def cen_peer(o):
         return {"cen": (c + o) % nc}
-
-    def a_peer(o):
-        q = (ga + o) % na
-        return {"pts": ((z // za) * za + q // nx) * nx + q % nx}
-
-    def b_peer(o):
-        return {"pts": (((gb + o) % zb) * za + z % za) * nx + x}
 
     def x_peer(o):
         return {"pts": z * nx + (x + o) % nx}
@@ -144,7 +132,7 @@
             return carry
         lax.fori_loop(first, last, body, 0)
 
-    for e in FAR + (1, -1):
+    for e in (3, -3, 1, -1):
         go_z(e, 0)
     x_near(0)
     load.wait()
@@ -154,10 +142,16 @@
         x_near(e)
     for e in (3, -3):
         gz_got(e).wait_recv()
+        go_z(-e, e)
         go_z(1, e)
         go_z(-1, e)
         x_near(e)
     x_on(0)
+    x_on(1)
+    x_on(-1)
+    for e in (2, -2, 4, -4):
+        gz_got(e).wait_recv()
+        x_near(e)
     for e in (6, -6):
         gz_got(e).wait_recv()
         go_z(1, e)
@@ -165,21 +159,16 @@
         if e == -6:
             go_z(2, e)
         x_near(e)
-    for e in (1, -1, 3, -3):
+    for e in (3, -3, 2, -2, 4, -4):
         x_on(e)
-    for e in (2, -2, 4, -4):
-        gz_got(e).wait_recv()
-        x_near(e)
-    x_on(6)
-    x_on(-6)
     for e in (5, -5, 7, -7, 8):
         gz_got(e).wait_recv()
         x_near(e)
     turns(d_blocks // 2, d_blocks)
     ahead = 3 * nx * chunk
     pts_t[n_d:n_d + ahead, :] = pts_t[:ahead, :]
-    for e in (2, -2, 4, -4):
-        x_on(e)
+    x_on(6)
+    x_on(-6)
 
     quarter = n_d // 4
     mine = z // (nz // 4)
@@ -295,20 +284,52 @@
     def add_down(v):
         return jnp.sum(v, axis=0, keepdims=True)
 
+    near = [(d, o) for d in (1, -1, 0) for o in range(nx) if d or o]
+    opposite = [(8, o) for o in range(nx)]
+
+    def col_copy(slot, d, o):
+        lane = (1 - d) * nx + o if d != 8 else 3 * nx + o
+        there = (1 - d) * nx + x if d != 8 else 3 * nx + x
+        return pltpu.make_async_remote_copy(
+            src_ref=cols_a.at[slot, nx + x], dst_ref=cols_a.at[slot, there],
+            send_sem=ca_send.at[slot, lane], recv_sem=ca_recv.at[slot, lane],
+            device_id={"pts": ((z + nz + d) % nz) * nx + (x + o) % nx}, device_id_type=MESH)
+
+    def centre_copy(slot, i, e):
+        return pltpu.make_async_remote_copy(
+            src_ref=cols_b.at[slot, 0], dst_ref=cols_b.at[slot, 1 + i],
+            send_sem=cb_send.at[slot, i], recv_sem=cb_recv.at[slot, i],
+            device_id=z_peer(e), device_id_type=MESH)
+
     def reduce_cols(slot):
-        start_a, wait_a = swap(cols_a.at[slot], slot, na, ga, a_peer, ca_send, ca_recv)
-        start_b, wait_b = swap(cols_b.at[slot], slot, zb, gb, b_peer, cb_send, cb_recv)
+        def first():
+            for d, o in opposite + near:
+                col_copy(slot, d, o).start()
 
         def middle():
-            wait_a()
-            cols_b[slot, gb] = total(cols_a.at[slot], na)
-            start_b()
+            for d, o in near:
+                col_copy(slot, d, o).wait_recv()
+            cols_b[slot, 0] = total(cols_a.at[slot], 3 * nx)
+            for i, e in enumerate(CENTRES):
+                centre_copy(slot, i, e).start()
 
         def last():
-            wait_b()
-            return total(cols_b.at[slot], zb)
-
-        return start_a, middle, last
+            for d, o in opposite:
+                col_copy(slot, d, o).wait_recv()
+            out = cols_a[slot, 3 * nx]
+            for i in range(1, nx):
+                out = out + cols_a[slot, 3 * nx + i]
+            for i, e in enumerate(CENTRES):
+                centre_copy(slot, i, e).wait_recv()
+            for i in range(len(CENTRES) + 1):
+                out = out + cols_b[slot, i]
+            for i, e in enumerate(CENTRES):
+                centre_copy(slot, i, e).wait_send()
+            for d, o in opposite + near:
+                col_copy(slot, d, o).wait_send()
+            return out
+
+        return first, middle, last
 
     for turn_no in range(PASSES):
         acc = [jnp.zeros((1, L), F32) for _ in range(col_tiles)]
@@ -319,7 +340,7 @@
                 mass[j * L:(j + 1) * L, t * L:(t + 1) * L] = m
                 acc[t] = acc[t] + add_down(m)
         for t in range(col_tiles):
-            cols_a[turn_no, ga, t:t + 1, :] = acc[t]
+            cols_a[turn_no, nx + x, t:t + 1, :] = acc[t]
         first, middle, last = reduce_cols(turn_no)
         first()
         middle()
@@ -346,7 +367,7 @@
     store = pltpu.make_async_copy(assign, assign_ref, local_sem.at[1])
     store.start()
     for t in range(col_tiles):
-        cols_a[PASSES, ga, t:t + 1, :] = acc[t]
+        cols_a[PASSES, nx + x, t:t + 1, :] = acc[t]
     first, middle, last = reduce_cols(PASSES)
     first()
 
@@ -372,7 +393,7 @@
             device_id=z_peer(VIA[e] if e in VIA else STEP[e]), device_id_type=MESH)
 
     block = nx * chunk
-    for first, n in PARTS:
+    def products(first, n):
         depth_rows = pl.ds(pl.multiple_of(((z + nz + first) % nz) * block, block), n * block)
         k = first + 7
 
@@ -413,8 +434,12 @@
         own[e + 7] = v
         rz(e).start()
 
+    products(*PARTS[0])
+    products(*PARTS[1])
     forward(*PARTS[0])
+    products(*PARTS[2])
     forward(*PARTS[1])
+    products(*PARTS[3])
     for i, (first, n) in enumerate(PARTS):
         for side in range(2):
             rx2(first, n, side).wait_recv()
@@ -424,6 +449,8 @@
                 rz(e).start()
         if i + 2 < len(PARTS):
             forward(*PARTS[i + 2])
+        if i == 0:
+            products(*PARTS[4])
         if i:
             before = PARTS[i - 1]
             for e in FEEDS:
@@ -448,16 +475,15 @@
     store.wait()
 
 
-def on_device(nx, nz, nc, za, points, centroids_t):
+def on_device(nx, nz, nc, points, centroids_t):
     n_rows, n_d = points.shape
     chunk, n_k = centroids_t.shape
-    na, zb = za * nx, nz // za
     rb, ct = n_rows // L, n_k // L
     assert nz == 16 and nx == 4
     vmem = pltpu.VMEM
     dma = pltpu.SemaphoreType.DMA
     return pl.pallas_call(
-        functools.partial(kernel, nx, nz, nc, za),
+        functools.partial(kernel, nx, nz, nc),
         out_shape=(
             jax.ShapeDtypeStruct((chunk, n_k), F32),
             jax.ShapeDtypeStruct((n_rows, n_k), BF16),
@@ -481,15 +507,15 @@
             vmem((nz, chunk, n_k), F32),
             vmem((nc, 2 * rb, L), F32),
             vmem((PASSES, nc, rb, L), F32),
-            vmem((PASSES + 1, na, ct, L), F32),
-            vmem((PASSES + 1, zb, ct, L), F32),
+            vmem((PASSES + 1, 4 * nx, ct, L), F32),
+            vmem((PASSES + 1, len(CENTRES) + 1, ct, L), F32),
             dma((2,)),
             dma((nz, 3)), dma((nz, 3)),
             dma((nz,)), dma((nz,)),
             dma((1, nc)), dma((1, nc)),
             dma((PASSES, nc)), dma((PASSES, nc)),
-            dma((PASSES + 1, na)), dma((PASSES + 1, na)),
-            dma((PASSES + 1, zb)), dma((PASSES + 1, zb)),
+            dma((PASSES + 1, 4 * nx)), dma((PASSES + 1, 4 * nx)),
+            dma((PASSES + 1, len(CENTRES))), dma((PASSES + 1, len(CENTRES))),
             dma((2, nz)), dma((2, nz)),
             dma((2, nz)), dma((2, nz)),
             dma((nz,)), dma((nz,)),
@@ -500,10 +526,10 @@
     )(points, centroids_t)
 
 
-def solution(mesh, nx=X_CHIPS, za=Z_GROUP):
+def solution(mesh, nx=X_CHIPS):
     nz = mesh.shape["pts"] // nx
     return jax.shard_map(
-        functools.partial(on_device, nx, nz, mesh.shape["cen"], za),
+        functools.partial(on_device, nx, nz, mesh.shape["cen"]),
         mesh=mesh,
         in_specs=(P("pts", None), P("pts", "cen")),
         out_specs=(P("pts", "cen"), P("pts", "cen")),

time: 146 us -> 136 us (0.932)
  the two profiles are of different devices: /device:TPU:32 before, /device:TPU:2 now
where the time goes in v5:
time: 136 us
  Pallas kernels  133 us (98%)
  local copies, waits for them, and re-layouts  2.7 us (2%)
    pallas_call x1, Pallas kernels, on_device(): pl.pallas_call(functools.partial(kernel, nx, nz, nc), out_shape=(jax.Shap...  133 us

profile of v5, /device:TPU:2, one launch (start us, length us, event | category | flops | bytes accessed | tf_op | source)
XLA Modules:
  0.0 136.2 jit_solution(10890028269316482209)
XLA Ops:
  0.6 0.0 copy-start
  0.6 0.7 copy-done
  1.4 132.8 %shard_map.41 = (f32[16,1024]{1,0:T(8,128)S(1)}, bf16[1024,1024]{1,0:T(8,128)(2,1)S(1)}) custom-call(bf16[1024,1024]{1,0:T(8,128)(2,1)} %points_ref.1, bf16[16,1024]{1,0:T(8,128)(2,1)S(1)} %copy-done), custom_call_target="tpu_custom_call" | custom-call | tf_op jit(solution)/shard_map/pallas_call | solution.py:485
  134.2 0.6 copy.6
  134.8 1.3 copy.7
Async XLA Ops:
  0.6 0.8 copy-start

commit v6 on v5

--- a/solution.py
+++ b/solution.py
@@ -49,6 +49,9 @@
 
     load = pltpu.make_async_copy(points_ref, pts, local_sem.at[0])
     load.start()
+    load_c = pltpu.make_async_copy(
+        cent_ref, piece.at[pl.ds(pl.multiple_of(p * chunk, chunk), chunk), :], local_sem.at[2])
+    load_c.start()
 
     barrier = pltpu.get_barrier_semaphore()
 
@@ -68,7 +71,6 @@
         first = ((z + nz + e) % nz) * nx + (x + nx + side) % nx
         return piece.at[pl.ds(pl.multiple_of(first * chunk, chunk), chunk), :]
 
-    piece[pl.ds(pl.multiple_of(p * chunk, chunk), chunk), :] = cent_ref[...]
 
     def gz(e, root):
         at = root - e + 7
@@ -132,6 +134,7 @@
             return carry
         lax.fori_loop(first, last, body, 0)
 
+    load_c.wait()
     for e in (3, -3, 1, -1):
         go_z(e, 0)
     x_near(0)
@@ -387,23 +390,31 @@
             send_sem=rx2_send.at[side, k], recv_sem=rx2_recv.at[side, k],
             device_id=x_peer(1 if side == 0 else nx - 1), device_id_type=MESH)
 
-    def rz(e):
-        return pltpu.make_async_remote_copy(
-            src_ref=own.at[e + 7], dst_ref=zrecv.at[e + 7], send_sem=rz_send.at[e + 7], recv_sem=rz_recv.at[e + 7],
-            device_id=z_peer(VIA[e] if e in VIA else STEP[e]), device_id_type=MESH)
+    def rz(f, h):
+        to = VIA[f] if f in VIA else STEP[f]
+        return pltpu.make_async_remote_copy(
+            src_ref=own.at[h, f + 7], dst_ref=zrecv.at[h, f + 7],
+            send_sem=rz_send.at[h, f + 7], recv_sem=rz_recv.at[h, f + 7],
+            device_id=z_peer(-to if h else to), device_id_type=MESH)
 
     block = nx * chunk
+    narrow = min(wide, half)
+
     def products(first, n):
-        depth_rows = pl.ds(pl.multiple_of(((z + nz + first) % nz) * block, block), n * block)
         k = first + 7
-
-        def product(t, carry):
-            where = pl.ds(pl.multiple_of(t * wide, wide), wide)
-            part = jnp.dot(pts_t[depth_rows, :], assign[:, where], preferred_element_type=F32)
-            prod[k:k + n, :, :, where] = part.reshape(n, nx, chunk, wide)
-            return carry
-
-        lax.fori_loop(0, tiles, product, 0)
+        for h in range(2):
+            lowest = 1 - first - n if h else first
+            depth_rows = pl.ds(pl.multiple_of(((z + nz + lowest) % nz) * block, block), n * block)
+
+            def product(t, carry):
+                where = pl.ds(pl.multiple_of(h * half + t * narrow, narrow), narrow)
+                part = jnp.dot(pts_t[depth_rows, :], assign[:, where], preferred_element_type=F32)
+                part = part.reshape(n, nx, chunk, narrow)
+                for i in range(n):
+                    prod[k + (n - 1 - i if h else i), :, :, where] = part[i]
+                return carry
+
+            lax.fori_loop(0, half // narrow, product, 0)
         for e in range(first, first + n):
             far = prod[e + 7, (x + 2) % nx].astype(BF16)
             xfar[0, e + 7] = far[:, :half]
@@ -426,13 +437,14 @@
                     xsend[side, e + 7, :, half:] = (v[:, half:] + w).astype(BF16)
             rx2(first, n, side).start()
 
-    def centre(e):
-        v = own[e + 7]
-        for f in FEEDS[e]:
-            rz(f).wait_recv()
-            v = v + zrecv[f + 7]
-        own[e + 7] = v
-        rz(e).start()
+    def centre(f):
+        for h in range(2):
+            v = own[h, f + 7]
+            for g in FEEDS[f]:
+                rz(g, h).wait_recv()
+                v = v + zrecv[h, g + 7]
+            own[h, f + 7] = v
+            rz(f, h).start()
 
     products(*PARTS[0])
     products(*PARTS[1])
@@ -444,9 +456,11 @@
         for side in range(2):
             rx2(first, n, side).wait_recv()
         for e in range(first, first + n):
-            own[e + 7] = prod[e + 7, x] + xrecv[0, e + 7].astype(F32) + xrecv[1, e + 7].astype(F32)
-            if e in VIA:
-                rz(e).start()
+            v = prod[e + 7, x] + xrecv[0, e + 7].astype(F32) + xrecv[1, e + 7].astype(F32)
+            for h in range(2):
+                own[h, e + 7] = v[:, h * half:(h + 1) * half]
+                if e in VIA:
+                    rz(e, h).start()
         if i + 2 < len(PARTS):
             forward(*PARTS[i + 2])
         if i == 0:
@@ -459,15 +473,18 @@
         else:
             middle()
     counts = last()
-    numer = own[7]
-    for e in (1, -1, 3, -3):
-        rz(e).wait_recv()
-        numer = numer + zrecv[e + 7]
-    for t in range(col_tiles):
-        newc_ref[:, t * L:(t + 1) * L] = numer[:, t * L:(t + 1) * L] / counts[t:t + 1, :]
-    for e in range(-7, 9):
-        if e:
-            rz(e).wait_send()
+    for h in range(2):
+        numer = own[h, 7]
+        for f in (1, -1, 3, -3):
+            rz(f, h).wait_recv()
+            numer = numer + zrecv[h, f + 7]
+        for t in range(col_tiles // 2):
+            u = h * (col_tiles // 2) + t
+            newc_ref[:, u * L:(u + 1) * L] = numer[:, t * L:(t + 1) * L] / counts[u:u + 1, :]
+    for h in range(2):
+        for f in range(-7, 9):
+            if f:
+                rz(f, h).wait_send()
     for first, n in PARTS:
         for side in range(2):
             rx1(first, n, side).wait_send()
@@ -488,7 +505,7 @@
             jax.ShapeDtypeStruct((chunk, n_k), F32),
             jax.ShapeDtypeStruct((n_rows, n_k), BF16),
         ),
-        in_specs=[pl.BlockSpec(memory_space=pl.ANY), pl.BlockSpec(memory_space=vmem)],
+        in_specs=[pl.BlockSpec(memory_space=pltpu.HBM), pl.BlockSpec(memory_space=pltpu.HBM)],
         out_specs=(pl.BlockSpec(memory_space=vmem), pl.BlockSpec(memory_space=pl.ANY)),
         scratch_shapes=[
             vmem((n_rows, n_d), BF16),
@@ -498,18 +515,18 @@
             vmem((1, n_k), F32),
             vmem((n_rows, L), F32),
             vmem((n_rows, n_k), BF16),
-            vmem((nz, chunk, n_k), F32),
+            vmem((2, nz, chunk, n_k // 2), F32),
             vmem((nz, nx, chunk, n_k), F32),
             vmem((2, nz, chunk, n_k // 2), BF16),
             vmem((2, nz, chunk, n_k // 2), BF16),
             vmem((2, nz, chunk, n_k), BF16),
             vmem((2, nz, chunk, n_k), BF16),
-            vmem((nz, chunk, n_k), F32),
+            vmem((2, nz, chunk, n_k // 2), F32),
             vmem((nc, 2 * rb, L), F32),
             vmem((PASSES, nc, rb, L), F32),
             vmem((PASSES + 1, 4 * nx, ct, L), F32),
             vmem((PASSES + 1, len(CENTRES) + 1, ct, L), F32),
-            dma((2,)),
+            dma((3,)),
             dma((nz, 3)), dma((nz, 3)),
             dma((nz,)), dma((nz,)),
             dma((1, nc)), dma((1, nc)),
@@ -518,7 +535,7 @@
             dma((PASSES + 1, len(CENTRES))), dma((PASSES + 1, len(CENTRES))),
             dma((2, nz)), dma((2, nz)),
             dma((2, nz)), dma((2, nz)),
-            dma((nz,)), dma((nz,)),
+            dma((2, nz)), dma((2, nz)),
         ],
         compiler_params=pltpu.CompilerParams(
             collective_id=0, has_side_effects=True, vmem_limit_bytes=50 * 1024 * 1024

time: 136 us -> 134 us (0.985)
  the two profiles are of different devices: /device:TPU:2 before, /device:TPU:32 now
where the time goes in v6:
time: 134 us; the launch traced here: 133 us
  Pallas kernels  130 us (97%)
  local copies, waits for them, and re-layouts  2.7 us (2%)
    pallas_call x1, Pallas kernels, on_device(): pl.pallas_call(functools.partial(kernel, nx, nz, nc), out_shape=(jax.Shap...  130 us
    unnamed x4, local copies, waits for them, and re-layouts  2.7 us

profile of v6, /device:TPU:32, one launch (start us, length us, event | category | flops | bytes accessed | tf_op | source)
XLA Modules:
  0.0 133.4 jit_solution(7482383707323621947)
XLA Ops:
  0.6 0.0 copy-start
  0.6 0.7 copy-done
  1.4 130.1 %shard_map.41 = (f32[16,1024]{1,0:T(8,128)S(1)}, bf16[1024,1024]{1,0:T(8,128)(2,1)S(1)}) custom-call(bf16[1024,1024]{1,0:T(8,128)(2,1)} %points_ref.1, bf16[16,1024]{1,0:T(8,128)(2,1)S(1)} %copy-done), custom_call_target="tpu_custom_call" | custom-call | tf_op jit(solution)/shard_map/pallas_call | solution.py:502
  131.5 0.6 copy.6
  132.1 1.3 copy.7
Async XLA Ops:
  0.6 0.8 copy-start

commit v7 on v6

--- a/solution.py
+++ b/solution.py
@@ -18,7 +18,7 @@
 STEP = {6: 3, -6: -3, 3: 3, -3: -3}
 GREET_Z = (1, -1, 2, -2, 3, -3)
 CENTRES = (6, -6, 3, -3)
-PARTS = ((5, 4), (-7, 3), (2, 3), (-4, 3), (-1, 3))
+PARTS = ((7, 2), (5, 2), (-7, 3), (2, 3), (-4, 3), (-1, 3))
 
 
 def kernel(nx, nz, nc, points_ref, cent_ref, newc_ref, assign_ref,
@@ -31,7 +31,7 @@
     chunk, n_k = cent_ref.shape
     row_blocks = n_rows // L
     col_tiles = n_k // L
-    wide = min(256, n_k)
+    wide = min(512, n_k)
 
     p = lax.axis_index("pts")
     c = lax.axis_index("cen")
@@ -238,15 +238,17 @@
                 src_ref=buf.at[me], dst_ref=buf.at[me], send_sem=send.at[slot, o],
                 recv_sem=recv.at[slot, o], device_id=peer(o), device_id_type=MESH)
 
-        def start(o, carry):
-            copy(o).start()
-            return carry
-
-        def wait(o, carry):
-            copy(o).wait()
-            return carry
-
-        return (lambda: lax.fori_loop(1, n, start, 0)), (lambda: lax.fori_loop(1, n, wait, 0))
+        def start():
+            for o in sorted(range(1, n), key=lambda o: abs(o - n // 2)):
+                copy(o).start()
+
+        def wait():
+            for o in range(1, n):
+                copy(o).wait_recv()
+            for o in range(1, n):
+                copy(o).wait_send()
+
+        return start, wait
 
     def total(buf, n):
         out = buf[0]
@@ -463,8 +465,8 @@
                     rz(e, h).start()
         if i + 2 < len(PARTS):
             forward(*PARTS[i + 2])
-        if i == 0:
-            products(*PARTS[4])
+        if i < 2:
+            products(*PARTS[4 + i])
         if i:
             before = PARTS[i - 1]
             for e in FEEDS:

time: 134 us -> 132 us (0.985)
  no operation moved by 1% of the time
where the time goes in v7:
time: 132 us
  Pallas kernels  129 us (98%)
  local copies, waits for them, and re-layouts  2.7 us (2%)
    pallas_call x1, Pallas kernels, on_device(): pl.pallas_call(functools.partial(kernel, nx, nz, nc), out_shape=(jax.Shap...  129 us
    unnamed x4, local copies, waits for them, and re-layouts  2.7 us

profile of v7, /device:TPU:32, one launch (start us, length us, event | category | flops | bytes accessed | tf_op | source)
XLA Modules:
  0.0 132.3 jit_solution(10967634539008894513)
XLA Ops:
  0.6 0.0 copy-start
  0.6 0.7 copy-done
  1.4 128.9 %shard_map.41 = (f32[16,1024]{1,0:T(8,128)S(1)}, bf16[1024,1024]{1,0:T(8,128)(2,1)S(1)}) custom-call(bf16[1024,1024]{1,0:T(8,128)(2,1)} %points_ref.1, bf16[16,1024]{1,0:T(8,128)(2,1)S(1)} %copy-done), custom_call_target="tpu_custom_call" | custom-call | tf_op jit(solution)/shard_map/pallas_call | solution.py:504
  130.3 0.6 copy.6
  130.9 1.3 copy.7
Async XLA Ops:
  0.6 0.8 copy-start
